TPU v7x, 512 devices: a whole 4x4x16 slice. The times are simulated.
512 devices in a mesh: dp: 64 (over y, z), tensor: 8 (over x, core).
Axes of the slice: x: 4, y: 4, z: 16, core: 2. Of those that a mesh axis runs over, the one named last changes fastest.
Arguments:
- grads: bfloat16 [64, 4096, 1024], P('dp', None, 'tensor'), may hold values from -70 to 70
- error: bfloat16 [64, 4096, 1024], P('dp', None, 'tensor'), may hold values from -3 to 3
- q_init: float32 [1024, 32], P('tensor'), may hold values from -6 to 6
Outputs:
- new_error: bfloat16 [64, 4096, 1024], P('dp', None, 'tensor')
- q_factor: float32 [1024, 32], P('tensor')
All inputs are finite; a program needn't handle non-finite values.
Results may differ from a plain program's by a relative error of at most 0.0059.
Values may be sent and summed in bfloat16 or wider, within the bound.
A program may use at most 64 MiB of HBM per device.

v0:
```python
import jax
import jax.numpy as jnp
from jax import lax
from jax.sharding import PartitionSpec as P

ITERS = 2


def triangular_basis(p_sum, gram_matrix):
    lower_factor = jnp.linalg.cholesky(gram_matrix)
    p_hat = lax.linalg.triangular_solve(
        lower_factor, p_sum, left_side=False, lower=True, transpose_a=True
    )
    return p_hat.astype(jnp.bfloat16)


def full_basis(p_sum):
    gram_matrix = jnp.dot(p_sum.T, p_sum, precision=lax.Precision.HIGHEST)
    return triangular_basis(p_sum, gram_matrix)


def on_device(grads, error, q_init):
    accumulated = (grads[0].astype(jnp.float32) + error[0].astype(jnp.float32)).astype(jnp.bfloat16)
    replicas = lax.axis_size("dp")
    q_factor = q_init
    p_basis = None
    for iteration in range(ITERS):
        partial_value = jnp.dot(
            accumulated, q_factor.astype(jnp.bfloat16), preferred_element_type=jnp.float32
        )
        p_sum = lax.psum(partial_value, ("dp", "tensor"))
        p_basis = full_basis(p_sum)
        q_partial = lax.dot_general(
            accumulated, p_basis, (((0,), (0,)), ((), ())), preferred_element_type=jnp.float32
        )
        q_factor = lax.psum(q_partial, "dp") / replicas
    approx = jnp.dot(p_basis.astype(jnp.float32), q_factor.T, precision=lax.Precision.HIGHEST)
    new_error = (accumulated.astype(jnp.float32) - approx).astype(jnp.bfloat16)[None]
    return (new_error, q_factor)


def solution(mesh):
    placed = (P("dp", None, "tensor"), P("dp", None, "tensor"), P("tensor", None))
    return jax.shard_map(
        on_device,
        mesh=mesh,
        in_specs=placed,
        out_specs=(P("dp", None, "tensor"), P("tensor", None)),
        check_vma=False,
    )
```

profile of v0, /device:TPU:4, one launch (start us, length us, event | category | flops | bytes accessed | tf_op | source)
XLA Modules:
  0.0 1506.2 jit_solution(17000493965865101748)
XLA Ops:
  7.2 0.0 copy-start.3
  7.2 0.0 all-reduce.3.cloned.1.call-start
  7.2 1.8 fusion.4
  9.0 0.0 copy-done.3
  9.0 1.3 fusion.15
  10.3 0.0 all-reduce.3.cloned.1.call-update
  10.3 0.0 all-reduce.5.cloned.1.call-start
  10.4 467.4 %all-reduce.3.cloned.1.call-done = f32[4096,32]{0,1:T(8,128)} async-done(((f32[4096,32]{0,1:T(8,128)}), f32[4096,32]{0,1:T(8,128)}) %all-reduce.3.cloned.1.call-update) | async-done | bytes 524304 | tf_op jit(solution)/shard_map/psum | solution.py:31
  477.8 0.0 copy-start
  477.8 1.8 fusion.18
  479.6 0.1 copy.5
  479.7 2.9 cholesky.44
  482.7 0.6 compare_reduce_fusion.1
  483.3 0.7 fusion.5
  484.0 2.4 custom-call.6
  486.4 0.0 copy-done
  486.4 0.7 fusion.2
  487.1 0.3 fusion.20
  487.4 275.6 %psum.29 = f32[128,32]{0,1:T(8,128)S(1)} all-reduce(f32[128,32]{0,1:T(8,128)S(1)} %fusion.20), channel_id=1, replica_groups=mesh['dp'=64,'tensor'=8] {'dp'}, use_global_device_ids=true, to_apply=%region_3.6 | all-reduce | flops 4096 | bytes 32768 | tf_op jit(solution)/shard_map/psum | solution.py:36
  762.9 1.3 fusion.13
  764.2 0.0 all-reduce.5.cloned.1.call-update
  764.2 447.8 %all-reduce.5.cloned.1.call-done = f32[4096,32]{0,1:T(8,128)} async-done(((f32[4096,32]{0,1:T(8,128)}), f32[4096,32]{0,1:T(8,128)}) %all-reduce.5.cloned.1.call-update) | async-done | bytes 524304 | tf_op jit(solution)/shard_map/psum | solution.py:31
  1212.0 0.0 copy-start.1
  1212.0 1.8 fusion.19
  1213.8 0.1 copy.6
  1213.9 2.9 cholesky.55
  1216.9 0.6 compare_reduce_fusion
  1217.5 0.7 fusion.6
  1218.2 2.4 custom-call.7
  1220.6 0.0 copy-done.1
  1220.6 0.7 fusion.3
  1221.3 0.3 fusion.21
  1221.5 275.6 %psum.31 = f32[128,32]{0,1:T(8,128)S(1)} all-reduce(f32[128,32]{0,1:T(8,128)S(1)} %fusion.21), channel_id=1, replica_groups=mesh['dp'=64,'tensor'=8] {'dp'}, use_global_device_ids=true, to_apply=%region_5.8 | all-reduce | flops 4096 | bytes 32768 | tf_op jit(solution)/shard_map/psum | solution.py:36
  1497.1 0.0 copy-start.2
  1497.1 2.2 fusion.1
  1499.4 0.0 copy-done.2
  (5 shorter events, 0.1 us)
Async XLA Ops:
  7.2 1.9 copy-start.3
  7.2 470.7 %all-reduce.3.cloned.1.call-start = ((), (), s32[]{:S(2)}) async-start(), calls=%async_computation | async-start | bytes 1048576 | tf_op jit(solution)/shard_map/psum | solution.py:31
  10.3 1201.7 %all-reduce.5.cloned.1.call-start = ((), (), s32[]{:S(2)}) async-start(), calls=%async_computation.1 | async-start | bytes 1048576 | tf_op jit(solution)/shard_map/psum | solution.py:31
  477.8 8.6 copy-start
  1212.0 8.6 copy-start.1
  1497.1 2.2 copy-start.2
Sparse Core Ops, SparseCore 0:
  14.0 463.7 all-reduce.2
  764.3 447.6 all-reduce.4
where the time goes:
time: 1510 us
  waiting for transfers between devices  915 us (61%)
  blocking collectives  551 us (36%)
  other arithmetic  15.2 us (1%)
    psum x2, waiting for transfers between devices, on_device(): p_sum = lax.psum(partial_value, ('dp', 'tensor'))  915 us
    psum x2, blocking collectives, on_device(): q_factor = lax.psum(q_partial, 'dp') / replicas  551 us
  transfers between devices with their start and end apart: 2, of which 2 were waited for; matrix products, arithmetic and copies ran while one was open for 0% of the time, Pallas kernels for 0%

commit v1 on v0

v1 whole, which is shorter than its diff:
```python
import functools

import jax
import jax.numpy as jnp
from jax import lax
from jax.experimental import pallas as pl
from jax.experimental.pallas import tpu as pltpu
from jax.sharding import PartitionSpec as P

MESH = pl.DeviceIdType.MESH
HIGHEST = lax.Precision.HIGHEST
ITERS = 2
RANK = 32
ROWS = 64
COLS = 128
TILES = 5
F32, BF16 = jnp.float32, jnp.bfloat16


def kernel(
    ny, nz, nt,
    grads, error, q_init, new_error, q_out,
    g_buf, e_buf, acc, y_buf, z_send, z_buf, a_sum, t_buf, send_tiles, r_buf, x_buf, out_tiles, p_own, p_all, m_buf,
    load_sem, y_send_sem, y_sem, z_send_sem, z_sem, t_send_sem, t_sem, r_send_sem, r_sem, x_send_sem, x_sem,
    o_send_sem, o_sem, pz_send_sem, pz_sem, py_send_sem, py_sem, store_sem,
):
    dp, t = lax.axis_index("dp"), lax.axis_index("tensor")
    y, z = lax.div(dp, nz), lax.rem(dp, nz)

    def remote(src, dst, send, recv, y_, z_, t_):
        return pltpu.make_async_remote_copy(
            src_ref=src, dst_ref=dst, send_sem=send, recv_sem=recv,
            device_id=(y_ * nz + z_, t_), device_id_type=MESH,
        )

    def got(ref, sem):
        remote(ref, ref, sem, sem, y, z, t).wait_recv()

    def sent(ref, sem):
        remote(ref, ref, sem, sem, y, z, t).wait_send()

    def y_peer(j):
        return lax.rem(y + j, ny)

    def z_peer(j):
        return lax.rem(z + j, nz)

    def t_peer(j):
        return lax.rem(t + j, nt)

    def target(i):
        half = lax.div(i + 1, 2)
        return lax.rem(z + nz // 2 + (1 - 2 * lax.rem(i, 2)) * half + nz, nz)

    def loads(i):
        zt = target(i)
        rows = pl.ds(pl.multiple_of(zt * (ny * ROWS), ny * ROWS), ny * ROWS)
        return (
            pltpu.make_async_copy(grads.at[0, rows, :], g_buf.at[i], load_sem.at[0, i]),
            pltpu.make_async_copy(error.at[0, rows, :], e_buf.at[i], load_sem.at[1, i]),
        )

    @pl.loop(0, nz)
    def _(i):
        for load in loads(i):
            load.start()

    barrier = pltpu.get_barrier_semaphore()
    for j in range(1, ny):
        pl.semaphore_signal(barrier, inc=1, device_id=(y_peer(j) * nz + z, t), device_id_type=MESH)
    for j in range(1, nz):
        pl.semaphore_signal(barrier, inc=1, device_id=(y * nz + z_peer(j), t), device_id_type=MESH)
    for j in range(1, nt):
        pl.semaphore_signal(barrier, inc=1, device_id=(dp, t_peer(j)), device_id_type=MESH)
    pl.semaphore_wait(barrier, (ny - 1) + (nz - 1) + (nt - 1))

    @pl.loop(0, nz)
    def _(i):
        for load in loads(i):
            load.wait()
        zt = target(i)
        total = (g_buf[i].astype(F32) + e_buf[i].astype(F32)).astype(BF16)
        acc[zt] = total.reshape(ny, ROWS, COLS)
        for j in range(1, ny):
            remote(acc.at[zt, y_peer(j)], y_buf.at[i, j - 1], y_send_sem, y_sem.at[i], y_peer(j), z, t).start()

    def y_total(i):
        got(y_buf.at[i], y_sem.at[i])
        total = acc[target(i), y].astype(F32)
        for j in range(ny - 1):
            total = total + y_buf[i, j].astype(F32)
        return total

    @pl.loop(0, nz - 1)
    def _(i):
        z_send[i] = y_total(i).astype(BF16)
        remote(z_send.at[i], z_buf.at[i], z_send_sem, z_sem, y, target(i), t).start()

    a_own = y_total(nz - 1)
    q_rows = q_init[...].T.astype(BF16)
    got(z_buf, z_sem)
    for i in range(nz - 1):
        a_own = a_own + z_buf[i].astype(F32)
    a_sum[...] = a_own

    lane16 = lax.broadcasted_iota(jnp.int32, (RANK // 2, 128), 1)
    lane32 = lax.broadcasted_iota(jnp.int32, (RANK, 128), 1)
    row32 = lax.broadcasted_iota(jnp.int32, (RANK, 128), 0)

    for it in range(ITERS):
        a = a_sum[...]
        a_high = a.astype(BF16)
        a_low = (a - a_high.astype(F32)).astype(BF16)
        parts = lax.dot_general(
            q_rows, jnp.concatenate([a_high, a_low], axis=0), (((1,), (1,)), ((), ())), preferred_element_type=F32
        )
        both = parts + pltpu.roll(parts, ROWS, 1)
        t_buf[it, t] = jnp.where(lane16 < ROWS, both[: RANK // 2], both[RANK // 2 :])
        for j in range(1, nt):
            remote(t_buf.at[it, t], t_buf.at[it, t], t_send_sem.at[it], t_sem.at[it], y, z, t_peer(j)).start()
        got(t_buf.at[it, pl.ds(0, nt - 1)], t_sem.at[it])
        p_packed = t_buf[it, 0]
        for j in range(1, nt):
            p_packed = p_packed + t_buf[it, j]
        p_rows = jnp.concatenate([p_packed, pltpu.roll(p_packed, ROWS, 1)], axis=0)[:, :ROWS]

        q_part = jnp.dot(p_rows, a, precision=HIGHEST, preferred_element_type=F32)
        gram_part = lax.dot_general(
            p_rows, p_rows, (((1,), (1,)), ((), ())), precision=HIGHEST, preferred_element_type=F32
        )
        for k in range(4):
            send_tiles[it, k] = q_part[8 * k : 8 * (k + 1)]
        send_tiles[it, 4] = jnp.concatenate([gram_part[8 * k : 8 * (k + 1)] for k in range(4)], axis=1)
        for k in range(TILES):
            zk = (k * nz) // TILES
            here = z == zk

            @pl.when(here)
            def _():
                r_buf[it, z] = send_tiles[it, k]

            @pl.when(jnp.logical_not(here))
            def _():
                remote(
                    send_tiles.at[it, k], r_buf.at[it, z], r_send_sem.at[it], r_sem.at[it], y, zk, t
                ).start()

        if it == ITERS - 1:
            p_own[...] = p_packed.astype(BF16)
            p_all[z, y] = p_own[...]

            @pl.loop(1, nz)
            def _(j):
                remote(p_own, p_all.at[z, y], pz_send_sem, pz_sem, y, z_peer(j), t).start()

        for k in range(TILES):
            zk = (k * nz) // TILES

            @pl.when(z == zk)
            def _():
                got(r_buf.at[it, pl.ds(0, nz - 1)], r_sem.at[it])
                total = r_buf[it, 0]
                for j in range(1, nz):
                    total = total + r_buf[it, j]
                x_buf[it, y] = total
                for j in range(1, ny):
                    remote(
                        x_buf.at[it, y], x_buf.at[it, y], x_send_sem.at[it], x_sem.at[it], y_peer(j), z, t
                    ).start()
                got(x_buf.at[it, pl.ds(0, ny - 1)], x_sem.at[it])
                total = x_buf[it, 0]
                for j in range(1, ny):
                    total = total + x_buf[it, j]
                out_tiles[it, k] = total
                for j in range(1, nz):
                    remote(
                        out_tiles.at[it, k], out_tiles.at[it, k], o_send_sem.at[it], o_sem.at[it, k], y, z_peer(j), t
                    ).start()

        if it == ITERS - 1:
            got(p_all.at[pl.ds(0, nz - 1), 0], pz_sem)
            for j in range(1, ny):
                remote(p_all.at[:, y], p_all.at[:, y], py_send_sem, py_sem, y_peer(j), z, t).start()

        for k in range(TILES):
            zk = (k * nz) // TILES

            @pl.when(z != zk)
            def _():
                got(out_tiles.at[it, k], o_sem.at[it, k])

        packed = out_tiles[it, 4]
        work = jnp.concatenate(
            [packed] + [pltpu.roll(packed, 128 - RANK * k, 1) for k in range(1, 4)], axis=0
        )
        lower = jnp.concatenate([out_tiles[it, k] for k in range(4)], axis=0)
        full = lower
        for k in range(RANK):
            column = jnp.broadcast_to(work[:, k : k + 1], (RANK, 128))
            inverse = 1.0 / column[k : k + 1]
            factor = jnp.where(row32 == k, 0.0, column * inverse)
            below = jnp.where(row32 > k, factor, 0.0)
            last = it == ITERS - 1
            if last:
                full = full - factor * full[k : k + 1]
            lower = lower - below * lower[k : k + 1]
            if k < RANK - 1:
                work = work - (factor if last else below) * work[k : k + 1]
        diagonal = jnp.sum(jnp.where(lane32 == row32, work, 0.0), axis=1, keepdims=True)
        q_next = lower / (jnp.sqrt(diagonal) * (ny * nz))
        q_rows = q_next.astype(BF16)
        if it == ITERS - 1:
            m = full / (diagonal * (ny * nz))
            q_out[...] = q_next.T

    m_high = m.astype(BF16)
    m_low = (m - m_high.astype(F32)).astype(BF16)
    half = RANK // 2
    m_buf[...] = jnp.concatenate(
        [
            jnp.concatenate([m_high[:half], m_high[half:]], axis=1),
            jnp.concatenate([m_low[:half], m_low[half:]], axis=1),
        ],
        axis=0,
    )
    got(p_all.at[:, pl.ds(0, ny - 1)], py_sem)

    @pl.loop(0, nz)
    def _(i):
        for yy in range(ny):
            tile = p_all[i, yy]
            doubled = jnp.concatenate([tile, tile], axis=0)
            product = lax.dot_general(
                doubled, m_buf[...], (((0,), (0,)), ((), ())), preferred_element_type=F32
            )
            approx = product[:ROWS, :COLS] + product[ROWS:, COLS:]
            g_buf[i, pl.ds(yy * ROWS, ROWS), :] = (acc[i, yy].astype(F32) - approx).astype(BF16)
        rows = pl.ds(pl.multiple_of(i * (ny * ROWS), ny * ROWS), ny * ROWS)
        pltpu.make_async_copy(g_buf.at[i], new_error.at[0, rows, :], store_sem).start()

    sent(acc.at[:, pl.ds(0, ny - 1)], y_send_sem)
    sent(z_send, z_send_sem)
    for it in range(ITERS):
        sent(t_buf.at[it, pl.ds(0, nt - 1)], t_send_sem.at[it])
        reducer = functools.reduce(jnp.logical_or, [z == (k * nz) // TILES for k in range(TILES)])

        @pl.when(reducer)
        def _():
            sent(send_tiles.at[it, pl.ds(0, TILES - 1)], r_send_sem.at[it])
            sent(x_buf.at[it, pl.ds(0, ny - 1)], x_send_sem.at[it])
            sent(r_buf.at[it, pl.ds(0, nz - 1)], o_send_sem.at[it])

        @pl.when(jnp.logical_not(reducer))
        def _():
            sent(send_tiles.at[it], r_send_sem.at[it])

    sent(p_all.at[pl.ds(0, nz - 1), 0], pz_send_sem)
    sent(p_all.at[:, pl.ds(0, ny - 1)], py_send_sem)
    pltpu.make_async_copy(g_buf, g_buf, store_sem).wait()


def on_device(ny, nz, nt, grads, error, q_init):
    rows = ny * nz * ROWS
    dma = pltpu.SemaphoreType.DMA
    return pl.pallas_call(
        functools.partial(kernel, ny, nz, nt),
        out_shape=(
            jax.ShapeDtypeStruct((1, rows, COLS), BF16),
            jax.ShapeDtypeStruct((COLS, RANK), F32),
        ),
        in_specs=[
            pl.BlockSpec(memory_space=pl.ANY),
            pl.BlockSpec(memory_space=pl.ANY),
            pl.BlockSpec(memory_space=pltpu.VMEM),
        ],
        out_specs=(pl.BlockSpec(memory_space=pl.ANY), pl.BlockSpec(memory_space=pltpu.VMEM)),
        scratch_shapes=[
            pltpu.VMEM((nz, ny * ROWS, COLS), BF16),
            pltpu.VMEM((nz, ny * ROWS, COLS), BF16),
            pltpu.VMEM((nz, ny, ROWS, COLS), BF16),
            pltpu.VMEM((nz, ny - 1, ROWS, COLS), BF16),
            pltpu.VMEM((nz - 1, ROWS, COLS), BF16),
            pltpu.VMEM((nz - 1, ROWS, COLS), BF16),
            pltpu.VMEM((ROWS, COLS), F32),
            pltpu.VMEM((ITERS, nt, RANK // 2, 128), F32),
            pltpu.VMEM((ITERS, TILES, 8, 128), F32),
            pltpu.VMEM((ITERS, nz, 8, 128), F32),
            pltpu.VMEM((ITERS, ny, 8, 128), F32),
            pltpu.VMEM((ITERS, TILES, 8, 128), F32),
            pltpu.VMEM((RANK // 2, 128), BF16),
            pltpu.VMEM((nz, ny, RANK // 2, 128), BF16),
            pltpu.VMEM((RANK, 2 * COLS), BF16),
            dma((2, nz)), dma, dma((nz,)), dma, dma, dma((ITERS,)), dma((ITERS,)), dma((ITERS,)), dma((ITERS,)),
            dma((ITERS,)), dma((ITERS,)), dma((ITERS,)), dma((ITERS, TILES)), dma, dma, dma, dma, dma,
        ],
        compiler_params=pltpu.CompilerParams(
            collective_id=0, has_side_effects=True, vmem_limit_bytes=32 * 1024 * 1024
        ),
    )(grads, error, q_init)


def solution(mesh, ny=4):
    nz, nt = mesh.shape["dp"] // ny, mesh.shape["tensor"]
    return jax.shard_map(
        functools.partial(on_device, ny, nz, nt),
        mesh=mesh,
        in_specs=(P("dp", None, "tensor"), P("dp", None, "tensor"), P("tensor", None)),
        out_specs=(P("dp", None, "tensor"), P("tensor", None)),
        check_vma=False,
    )
```

time: 1510 us -> 97.6 us (0.06)
  the two profiles are of different devices: /device:TPU:4 before, /device:TPU:1 now
where the time goes in v1:
time: 97.6 us; the launch traced here: 95.9 us
  Pallas kernels  90.3 us (93%)
  local copies, waits for them, and re-layouts  4.91 us (5%)
    pallas_call x1, Pallas kernels, on_device(): pl.pallas_call(functools.partial(kernel, ny, nz, nt), out_shape=(jax.Shap...  90.3 us
    unnamed x6, local copies, waits for them, and re-layouts  4.23 us

profile of v1, /device:TPU:1, one launch (start us, length us, event | category | flops | bytes accessed | tf_op | source)
XLA Modules:
  0.0 95.9 jit_solution(11548444751574384026)
XLA Ops:
  0.6 0.8 copy.5.q_init
  1.4 0.0 copy-start
  1.5 1.2 %copy-done = bf16[1,4096,128]{2,1,0:T(8,128)(2,1)S(1)} copy-done((bf16[1,4096,128]{2,1,0:T(8,128)(2,1)S(1)}, bf16[1,4096,128]{2,1,0:T(8,128)(2,1)}, u32[]{:S(2)}) %copy-start) | copy-done | bytes 1048600
  2.7 0.0 copy-start.1
  2.7 1.2 %copy-done.1 = bf16[1,4096,128]{2,1,0:T(8,128)(2,1)S(1)} copy-done((bf16[1,4096,128]{2,1,0:T(8,128)(2,1)S(1)}, bf16[1,4096,128]{2,1,0:T(8,128)(2,1)}, u32[]{:S(2)}) %copy-start.1) | copy-done | bytes 1048600
  3.9 90.3 %shard_map.50 = (bf16[1,4096,128]{2,1,0:T(8,128)(2,1)S(1)}, f32[128,32]{1,0:T(8,128)S(1)}) custom-call(bf16[1,4096,128]{2,1,0:T(8,128)(2,1)S(1)} %copy-done, bf16[1,4096,128]{2,1,0:T(8,128)(2,1)S(1)} %copy-done.1, f32[128,32]{1,0:T(8,128)S(1)} %copy.5.q_init), custom_call_target="tpu_custom_call" | custom-call | tf_op jit(solution)/shard_map/pallas_call | solution.py:265
  94.2 0.7 copy.6
  94.9 1.0 %copy.8 = bf16[1,4096,128]{2,1,0:T(8,128)(2,1)} copy(bf16[1,4096,128]{2,1,0:T(8,128)(2,1)S(1)} %get-tuple-element.6) | data formatting | bytes 2097152
Async XLA Ops:
  1.4 1.2 %copy-start = (bf16[1,4096,128]{2,1,0:T(8,128)(2,1)S(1)}, bf16[1,4096,128]{2,1,0:T(8,128)(2,1)}, u32[]{:S(2)}) copy-start(bf16[1,4096,128]{2,1,0:T(8,128)(2,1)} %grads.1) | copy-start | bytes 3145732
  2.7 1.2 %copy-start.1 = (bf16[1,4096,128]{2,1,0:T(8,128)(2,1)S(1)}, bf16[1,4096,128]{2,1,0:T(8,128)(2,1)}, u32[]{:S(2)}) copy-start(bf16[1,4096,128]{2,1,0:T(8,128)(2,1)} %error.1) | copy-start | bytes 3145732

commit v2 on v0

v2 whole, which is shorter than its diff:
```python
import functools

import jax
import jax.numpy as jnp
from jax import lax
from jax.experimental import pallas as pl
from jax.experimental.pallas import tpu as pltpu
from jax.sharding import PartitionSpec as P

MESH = pl.DeviceIdType.MESH
HIGHEST = lax.Precision.HIGHEST
RANK = 32
BLOCK = 64
PARTS = 2
PART = BLOCK // PARTS
GROUP = 4
COLS = 128
SUMS = 40
F32, BF16 = jnp.float32, jnp.bfloat16


def eliminate(gram_packed, right, both_sides):
    row = lax.broadcasted_iota(jnp.int32, (RANK, 128), 0)
    lane = lax.broadcasted_iota(jnp.int32, (RANK, 128), 1)
    work = jnp.concatenate(
        [gram_packed] + [pltpu.roll(gram_packed, 128 - RANK * k, 1) for k in range(1, RANK // 8)], axis=0
    )
    lower, full = right, right
    for k in range(RANK):
        column = jnp.broadcast_to(work[:, k : k + 1], (RANK, 128))
        inverse = 1.0 / column[k : k + 1]
        factor = jnp.where(row == k, 0.0, column * inverse)
        below = jnp.where(row > k, factor, 0.0)
        if both_sides:
            full = full - factor * full[k : k + 1]
        lower = lower - below * lower[k : k + 1]
        if k < RANK - 1:
            work = work - (factor if both_sides else below) * work[k : k + 1]
    diagonal = jnp.sum(jnp.where(lane == row, work, 0.0), axis=1, keepdims=True)
    return diagonal, lower, full


def kernel(
    ny, nz, nt,
    grads, error, q_init, new_error, q_out,
    g_buf, e_buf, acc, y_buf, z_send, z_buf, a_all, t_buf, p1_all, s_buf, part_buf, c_buf, x_buf, p2_all, p_rows,
    load_sem, y_send_sem, y_sem, z_send_sem, z_sem, a_send_sem, a_sem, t_send_sem, t_sem, p_send_sem, p_sem,
    s_send_sem, s_sem, c_send_sem, c_sem, x_send_sem, x_sem, store_sem,
):
    nx = nt // 2
    dp, t = lax.axis_index("dp"), lax.axis_index("tensor")
    y, z = lax.div(dp, nz), lax.rem(dp, nz)
    x, core = lax.div(t, 2), lax.rem(t, 2)
    other = 1 - core
    sibling = x * 2 + other
    half = nz * BLOCK // 2

    def remote(src, dst, send, recv, y_, z_, t_):
        return pltpu.make_async_remote_copy(
            src_ref=src, dst_ref=dst, send_sem=send, recv_sem=recv,
            device_id=(y_ * nz + z_, t_), device_id_type=MESH,
        )

    def got(ref, sem):
        remote(ref, ref, sem, sem, y, z, t).wait_recv()

    def sent(ref, sem):
        remote(ref, ref, sem, sem, y, z, t).wait_send()

    def y_peer(j):
        return lax.rem(y + j, ny)

    def t_peer(j):
        return lax.rem(t + j, nt)

    def target(i):
        return lax.rem(z + nz // 2 + (1 - 2 * lax.rem(i, 2)) * lax.div(i + 1, 2) + nz, nz)

    def loads(i):
        zt = target(i)
        return (
            pltpu.make_async_copy(grads.at[:, zt], g_buf.at[i], load_sem.at[0, i]),
            pltpu.make_async_copy(error.at[:, zt], e_buf.at[i], load_sem.at[1, i]),
        )

    barrier = pltpu.get_barrier_semaphore()

    @pl.loop(0, nz - 1)
    def _(i):
        pl.semaphore_signal(barrier, inc=1, device_id=(y * nz + target(i), t), device_id_type=MESH)

    for j in range(1, ny):
        pl.semaphore_signal(barrier, inc=1, device_id=(y_peer(j) * nz + z, t), device_id_type=MESH)
    for j in range(1, nt):
        pl.semaphore_signal(barrier, inc=1, device_id=(dp, t_peer(j)), device_id_type=MESH)

    @pl.loop(0, nz)
    def _(i):
        for load in loads(i):
            load.start()

    at_the_end = []

    def rows_of(h):
        return pl.ds(h * PART, PART)

    def send_y(h, g):
        group = pl.ds(g * GROUP, GROUP)
        for j in range(1, ny):
            remote(
                acc.at[group, y_peer(j), rows_of(h)], y_buf.at[h, group, j - 1],
                y_send_sem, y_sem.at[h, g], y_peer(j), z, t,
            ).start()

    def accumulate(g):
        @pl.loop(g * GROUP, (g + 1) * GROUP)
        def _(i):
            for load in loads(i):
                load.wait()
            acc[i] = (g_buf[i].astype(F32) + e_buf[i].astype(F32)).astype(BF16)

    accumulate(0)
    pl.semaphore_wait(barrier, (ny - 1) + (nz - 1) + (nt - 1))
    send_y(0, 0)

    @pl.loop(1, nz // GROUP)
    def _(g):
        accumulate(g)
        send_y(0, g)

    for h in range(1, PARTS):

        @pl.loop(0, nz // GROUP)
        def _(g):
            send_y(h, g)

    at_the_end.append(lambda: sent(acc.at[:, pl.ds(0, ny - 1)], y_send_sem))

    def y_total(h, i):
        total = acc[i, y, h * PART : (h + 1) * PART].astype(F32)
        for j in range(ny - 1):
            total = total + y_buf[h, i, j].astype(F32)
        return total

    own = []
    for h in range(PARTS):

        @pl.loop(0, nz // GROUP)
        def _(g):
            got(y_buf.at[h, pl.ds(g * GROUP, GROUP)], y_sem.at[h, g])

            @pl.loop(g * GROUP, lax.min((g + 1) * GROUP, nz - 1))
            def _(i):
                z_send[h, i] = y_total(h, i).astype(BF16)
                remote(z_send.at[h, i], z_buf.at[h, i], z_send_sem, z_sem.at[h], y, target(i), t).start()

        own.append(y_total(h, nz - 1))
    at_the_end.append(lambda: sent(z_send, z_send_sem))

    for h in range(PARTS):
        got(z_buf.at[h], z_sem.at[h])
        total = own[h]
        for i in range(nz - 1):
            total = total + z_buf[h, i].astype(F32)
        a_all[z, h * PART : (h + 1) * PART] = total.astype(BF16)
        mine = a_all.at[z, rows_of(h)]

        @pl.loop(0, nz - 1)
        def _(i):
            remote(mine, mine, a_send_sem, a_sem, y, target(i), t).start()

    at_the_end.append(lambda: sent(a_all.at[pl.ds(0, nz - 1)], a_send_sem))

    lane16 = lax.broadcasted_iota(jnp.int32, (RANK // 2, 128), 1)
    q_rows = q_init[...].astype(BF16)
    block = a_all[z]
    p_part = lax.dot_general(
        q_rows, jnp.concatenate([block, block], axis=0), (((1,), (1,)), ((), ())), preferred_element_type=F32
    )
    t_buf[t] = jnp.where(lane16 < BLOCK, p_part[: RANK // 2], p_part[RANK // 2 :])
    for j in range(1, nt):
        remote(t_buf.at[t], t_buf.at[t], t_send_sem, t_sem, y, z, t_peer(j)).start()
    at_the_end.append(lambda: sent(t_buf.at[pl.ds(0, nt - 1)], t_send_sem))
    got(t_buf.at[pl.ds(0, nt - 1)], t_sem)
    p_packed = t_buf[0]
    for j in range(1, nt):
        p_packed = p_packed + t_buf[j]
    p1_all[z] = p_packed.astype(BF16)

    @pl.loop(0, nz - 1)
    def _(i):
        remote(p1_all.at[z], p1_all.at[z], p_send_sem, p_sem, y, target(i), t).start()

    at_the_end.append(lambda: sent(p1_all.at[pl.ds(0, nz - 1)], p_send_sem))
    got(a_all.at[pl.ds(0, nz - 1)], a_sem)
    got(p1_all.at[pl.ds(0, nz - 1)], p_sem)
    a = a_all[...].reshape(nz * BLOCK, COLS)
    columns = []
    for m in range(nz // 2):
        first, second = p1_all[2 * m].astype(F32), p1_all[2 * m + 1].astype(F32)
        top = jnp.where(lane16 < BLOCK, first, pltpu.roll(second, BLOCK, 1))
        bottom = jnp.where(lane16 < BLOCK, pltpu.roll(first, BLOCK, 1), second)
        columns.append(jnp.concatenate([top, bottom], axis=0))
    p1 = jnp.concatenate(columns, axis=1).astype(BF16)

    def sum_over_y(it, q_part, gram_part):
        s_buf[it, y, :RANK] = q_part
        s_buf[it, y, RANK:] = jnp.concatenate([gram_part[8 * k : 8 * (k + 1)] for k in range(RANK // 8)], axis=1)
        for j in range(1, ny):
            remote(s_buf.at[it, y], s_buf.at[it, y], s_send_sem.at[it], s_sem.at[it], y_peer(j), z, t).start()
        at_the_end.append(lambda: sent(s_buf.at[it, pl.ds(0, ny - 1)], s_send_sem.at[it]))

    def summed_over_y(it):
        got(s_buf.at[it, pl.ds(0, ny - 1)], s_sem.at[it])
        total = s_buf[it, 0]
        for j in range(1, ny):
            total = total + s_buf[it, j]
        return total[:RANK], total[RANK:]

    sum_over_y(
        0,
        jnp.dot(p1, a, preferred_element_type=F32),
        lax.dot_general(p1, p1, (((1,), (1,)), ((), ())), preferred_element_type=F32),
    )
    right, gram = summed_over_y(0)
    diagonal, lower, _ = eliminate(gram, right, False)
    q_rows = (lower / (jnp.sqrt(diagonal) * (ny * nz))).astype(BF16)

    p_part = lax.dot_general(q_rows, a, (((1,), (1,)), ((), ())), preferred_element_type=F32)
    part_buf[0] = p_part[:, :half]
    part_buf[1] = p_part[:, half:]
    remote(part_buf.at[other], c_buf, c_send_sem.at[0], c_sem.at[0], y, z, sibling).start()
    at_the_end.append(lambda: sent(c_buf, c_send_sem.at[0]))
    got(c_buf, c_sem.at[0])
    x_buf[x] = part_buf[core] + c_buf[...]
    for j in range(1, nx):
        remote(x_buf.at[x], x_buf.at[x], x_send_sem, x_sem, y, z, lax.rem(x + j, nx) * 2 + core).start()
    at_the_end.append(lambda: sent(x_buf.at[pl.ds(0, nx - 1)], x_send_sem))
    got(x_buf.at[pl.ds(0, nx - 1)], x_sem)
    p_half = x_buf[0]
    for j in range(1, nx):
        p_half = p_half + x_buf[j]
    p2_all[y, core] = p_half
    mine = p2_all.at[y, core]
    remote(mine, mine, c_send_sem.at[1], c_sem.at[1], y, z, sibling).start()
    at_the_end.append(lambda: sent(c_buf, c_send_sem.at[1]))
    for j in range(1, ny):
        remote(mine, mine, s_send_sem.at[2], s_sem.at[2], y_peer(j), z, t).start()
    at_the_end.append(lambda: sent(p2_all.at[pl.ds(0, ny - 1), 0], s_send_sem.at[2]))
    got(p2_all.at[y, other], c_sem.at[1])
    p2 = jnp.concatenate([p2_all[y, 0], p2_all[y, 1]], axis=1)
    p2_high = p2.astype(BF16)
    p2_low = (p2 - p2_high.astype(F32)).astype(BF16)
    both = jnp.dot(jnp.concatenate([p2_high, p2_low], axis=0), a, preferred_element_type=F32)
    sum_over_y(
        1,
        both[:RANK] + both[RANK:],
        lax.dot_general(p2, p2, (((1,), (1,)), ((), ())), precision=HIGHEST, preferred_element_type=F32),
    )

    got(p2_all.at[pl.ds(0, ny - 1), 0], s_sem.at[2])
    for j in range(1, ny):
        theirs = p2_all.at[y_peer(j), core]
        remote(theirs, theirs, c_send_sem.at[2], c_sem.at[2], y, z, sibling).start()
    at_the_end.append(lambda: sent(p2_all.at[pl.ds(0, ny - 1), 0], c_send_sem.at[2]))
    right, gram = summed_over_y(1)
    got(p2_all.at[pl.ds(0, ny - 1), 0], c_sem.at[2])

    for yy in range(ny):
        for c in range(2):

            @pl.loop(0, half // 128)
            def _(b):
                tile = p2_all[yy, c, :, pl.ds(pl.multiple_of(b * 128, 128), 128)]
                high = tile.astype(BF16)
                low = (tile - high.astype(F32)).astype(BF16)
                start = yy * 2 * half + c * half + b * 128
                p_rows[pl.ds(pl.multiple_of(start, 128), 128)] = jnp.concatenate([high, low, high, low], axis=0).T

    diagonal, lower, full = eliminate(gram, right, True)
    q_out[...] = lower / (jnp.sqrt(diagonal) * (ny * nz))
    m = full / (diagonal * (ny * nz))
    m_high = m.astype(BF16)
    m_low = (m - m_high.astype(F32)).astype(BF16)
    m_rows = jnp.concatenate([m_high, m_high, m_low, m_low], axis=0)

    @pl.loop(0, nz)
    def _(i):
        zt = target(i)
        left = jnp.concatenate(
            [p_rows[pl.ds(pl.multiple_of((yy * nz + zt) * BLOCK, BLOCK), BLOCK)] for yy in range(ny)], axis=0
        )
        approx = jnp.dot(left, m_rows, preferred_element_type=F32).reshape(ny, BLOCK, COLS)
        g_buf[i] = (acc[i].astype(F32) - approx).astype(BF16)
        pltpu.make_async_copy(g_buf.at[i], new_error.at[:, zt], store_sem).start()

    for wait in at_the_end:
        wait()
    pltpu.make_async_copy(g_buf, g_buf, store_sem).wait()


def on_device(ny, nz, nt, grads, error, q_init):
    dma = pltpu.SemaphoreType.DMA
    blocks = (ny, nz, BLOCK, COLS)
    half = nz * BLOCK // 2
    new_error, q_rows = pl.pallas_call(
        functools.partial(kernel, ny, nz, nt),
        out_shape=(jax.ShapeDtypeStruct(blocks, BF16), jax.ShapeDtypeStruct((RANK, COLS), F32)),
        in_specs=[
            pl.BlockSpec(memory_space=pl.ANY),
            pl.BlockSpec(memory_space=pl.ANY),
            pl.BlockSpec(memory_space=pltpu.VMEM),
        ],
        out_specs=(pl.BlockSpec(memory_space=pl.ANY), pl.BlockSpec(memory_space=pltpu.VMEM)),
        scratch_shapes=[
            pltpu.VMEM((nz, ny, BLOCK, COLS), BF16),
            pltpu.VMEM((nz, ny, BLOCK, COLS), BF16),
            pltpu.VMEM((nz, ny, BLOCK, COLS), BF16),
            pltpu.VMEM((PARTS, nz, ny - 1, PART, COLS), BF16),
            pltpu.VMEM((PARTS, nz - 1, PART, COLS), BF16),
            pltpu.VMEM((PARTS, nz - 1, PART, COLS), BF16),
            pltpu.VMEM((nz, BLOCK, COLS), BF16),
            pltpu.VMEM((nt, RANK // 2, 128), F32),
            pltpu.VMEM((nz, RANK // 2, 128), BF16),
            pltpu.VMEM((2, ny, SUMS, 128), F32),
            pltpu.VMEM((2, RANK, half), F32),
            pltpu.VMEM((RANK, half), F32),
            pltpu.VMEM((nt // 2, RANK, half), F32),
            pltpu.VMEM((ny, 2, RANK, half), F32),
            pltpu.VMEM((ny * nz * BLOCK, 4 * RANK), BF16),
            dma((2, nz)), dma, dma((PARTS, nz // GROUP)), dma, dma((PARTS,)), dma, dma, dma, dma, dma, dma,
            dma((3,)), dma((3,)), dma((3,)), dma((3,)), dma, dma, dma,
        ],
        compiler_params=pltpu.CompilerParams(
            collective_id=0, has_side_effects=True, vmem_limit_bytes=60 * 1024 * 1024
        ),
    )(grads.reshape(blocks), error.reshape(blocks), q_init.T)
    return new_error.reshape(1, ny * nz * BLOCK, COLS), q_rows.T


def solution(mesh, ny=4):
    nz, nt = mesh.shape["dp"] // ny, mesh.shape["tensor"]
    return jax.shard_map(
        functools.partial(on_device, ny, nz, nt),
        mesh=mesh,
        in_specs=(P("dp", None, "tensor"), P("dp", None, "tensor"), P("tensor", None)),
        out_specs=(P("dp", None, "tensor"), P("tensor", None)),
        check_vma=False,
    )
```

time: 1510 us -> 84.7 us (0.06)
  the two profiles are of different devices: /device:TPU:4 before, /device:TPU:1 now
where the time goes in v2:
time: 84.7 us; the launch traced here: 84.5 us
  Pallas kernels  81 us (96%)
  local copies, waits for them, and re-layouts  2.88 us (3%)
    pallas_call x1, Pallas kernels, on_device(): pl.pallas_call(functools.partial(kernel, ny, nz, nt), out_shape=(jax.Shap...  81 us
    unnamed x4, local copies, waits for them, and re-layouts  2.88 us

profile of v2, /device:TPU:1, one launch (start us, length us, event | category | flops | bytes accessed | tf_op | source)
XLA Modules:
  0.0 84.5 jit_solution(6511939912946681616)
XLA Ops:
  0.6 81.0 %shard_map.50 = (bf16[4,16,64,128]{3,2,1,0:T(8,128)(2,1)}, f32[32,128]{1,0:T(8,128)}) custom-call(bf16[4,16,64,128]{3,2,1,0:T(8,128)(2,1)} %bitcast.5, bf16[4,16,64,128]{3,2,1,0:T(8,128)(2,1)} %bitcast.6, f32[32,128]{1,0:T(8,128)} %bitcast.8), custom_call_target="tpu_custom_call" | custom-call | tf_op jit(solution)/shard_map/pallas_call | solution.py:306
  81.6 0.0 copy-start
  81.6 2.3 %copy.7 = bf16[1,4096,128]{2,1,0:T(8,128)(2,1)} copy(bf16[1,4096,128]{2,1,0:T(8,128)(2,1)} %bitcast.7) | data formatting | bytes 2097152
  83.9 0.0 copy-done
  83.9 0.6 copy.8
Async XLA Ops:
  81.6 2.3 %copy-start = (f32[32,128]{1,0:T(8,128)S(1)}, f32[32,128]{1,0:T(8,128)}, u32[]{:S(2)}) copy-start(f32[32,128]{1,0:T(8,128)} %get-tuple-element.5) | copy-start | bytes 49156

commit v3 on v2

--- a/solution.py
+++ b/solution.py
@@ -13,31 +13,51 @@
 BLOCK = 64
 PARTS = 2
 PART = BLOCK // PARTS
-GROUP = 4
+STEPS = 8
+GROUP = 2
 COLS = 128
 SUMS = 40
 F32, BF16 = jnp.float32, jnp.bfloat16
 
 
 def eliminate(gram_packed, right, both_sides):
-    row = lax.broadcasted_iota(jnp.int32, (RANK, 128), 0)
-    lane = lax.broadcasted_iota(jnp.int32, (RANK, 128), 1)
-    work = jnp.concatenate(
-        [gram_packed] + [pltpu.roll(gram_packed, 128 - RANK * k, 1) for k in range(1, RANK // 8)], axis=0
-    )
-    lower, full = right, right
-    for k in range(RANK):
-        column = jnp.broadcast_to(work[:, k : k + 1], (RANK, 128))
-        inverse = 1.0 / column[k : k + 1]
-        factor = jnp.where(row == k, 0.0, column * inverse)
-        below = jnp.where(row > k, factor, 0.0)
-        if both_sides:
-            full = full - factor * full[k : k + 1]
-        lower = lower - below * lower[k : k + 1]
-        if k < RANK - 1:
-            work = work - (factor if both_sides else below) * work[k : k + 1]
-    diagonal = jnp.sum(jnp.where(lane == row, work, 0.0), axis=1, keepdims=True)
-    return diagonal, lower, full
+    row = lax.broadcasted_iota(jnp.int32, (8, 128), 0)
+    lane = lax.broadcasted_iota(jnp.int32, (8, 128), 1)
+    tiles = RANK // 8
+    work = [gram_packed if r == 0 else pltpu.roll(gram_packed, 128 - RANK * r, 1) for r in range(tiles)]
+    lower = [right[8 * r : 8 * (r + 1)] for r in range(tiles)]
+    full = list(lower)
+    diagonal = [jnp.zeros((8, 128), F32)] * tiles
+    for first in range(0, RANK, STEPS):
+        columns = [
+            [jnp.broadcast_to(work[r][:, first + j : first + j + 1], (8, 128)) for r in range(tiles)]
+            for j in range(STEPS)
+        ]
+        for j in range(STEPS):
+            k = first + j
+            own, at = k // 8, k % 8
+            pivot = columns[j][own][at : at + 1]
+            inverse = 1.0 / pivot
+            diagonal[own] = jnp.where(row == at, pivot, diagonal[own])
+            factor, below = [], []
+            for r in range(tiles):
+                scaled = columns[j][r] * inverse
+                factor.append(jnp.where(row == at, 0.0, scaled) if r == own else scaled)
+                below.append(jnp.where(row > at, scaled, 0.0) if r == own else scaled)
+
+            def step(matrix, factors, start):
+                pivot_row = matrix[own][at : at + 1]
+                for r in range(start, tiles):
+                    matrix[r] = matrix[r] - factors[r] * pivot_row
+
+            both = (factor, 0) if both_sides else (below, own)
+            for later in columns[j + 1 :]:
+                step(later, *both)
+            step(lower, below, own)
+            if both_sides:
+                step(full, factor, 0)
+            step(work, *both)
+    return tuple(jnp.concatenate(m, axis=0) for m in (diagonal, lower, full))
 
 
 def kernel(
@@ -45,7 +65,7 @@
     grads, error, q_init, new_error, q_out,
     g_buf, e_buf, acc, y_buf, z_send, z_buf, a_all, t_buf, p1_all, s_buf, part_buf, c_buf, x_buf, p2_all, p_rows,
     load_sem, y_send_sem, y_sem, z_send_sem, z_sem, a_send_sem, a_sem, t_send_sem, t_sem, p_send_sem, p_sem,
-    s_send_sem, s_sem, c_send_sem, c_sem, x_send_sem, x_sem, store_sem,
+    s_send_sem, s_sem, c_send_sem, c_sem, x_send_sem, x_sem, store_sem, ready,
 ):
     nx = nt // 2
     dp, t = lax.axis_index("dp"), lax.axis_index("tensor")
@@ -85,14 +105,18 @@
 
     barrier = pltpu.get_barrier_semaphore()
 
+    def enter(y_, z_, t_):
+        pl.semaphore_signal(barrier, inc=1, device_id=(y_ * nz + z_, t_), device_id_type=MESH)
+
     @pl.loop(0, nz - 1)
     def _(i):
-        pl.semaphore_signal(barrier, inc=1, device_id=(y * nz + target(i), t), device_id_type=MESH)
+        enter(y, target(i), x * 2 + 1)
 
     for j in range(1, ny):
-        pl.semaphore_signal(barrier, inc=1, device_id=(y_peer(j) * nz + z, t), device_id_type=MESH)
-    for j in range(1, nt):
-        pl.semaphore_signal(barrier, inc=1, device_id=(dp, t_peer(j)), device_id_type=MESH)
+        enter(y_peer(j), z, x * 2)
+    for j in range(1, nx):
+        enter(y, z, lax.rem(x + j, nx) * 2 + 1)
+    enter(y, z, sibling)
 
     @pl.loop(0, nz)
     def _(i):
@@ -120,7 +144,18 @@
             acc[i] = (g_buf[i].astype(F32) + e_buf[i].astype(F32)).astype(BF16)
 
     accumulate(0)
-    pl.semaphore_wait(barrier, (ny - 1) + (nz - 1) + (nt - 1))
+
+    def entered(here, count):
+        @pl.when(core == here)
+        def _():
+            pl.semaphore_wait(barrier, count)
+            pl.semaphore_signal(ready, inc=1, device_id=(dp, sibling), device_id_type=MESH)
+
+        @pl.when(core != here)
+        def _():
+            pl.semaphore_wait(ready, 1)
+
+    entered(0, 2 * (ny - 1) + 1)
     send_y(0, 0)
 
     @pl.loop(1, nz // GROUP)
@@ -142,6 +177,7 @@
             total = total + y_buf[h, i, j].astype(F32)
         return total
 
+    entered(1, 2 * (nz - 1) + 2 * (nx - 1) + 1)
     own = []
     for h in range(PARTS):
 
@@ -258,6 +294,17 @@
         lax.dot_general(p2, p2, (((1,), (1,)), ((), ())), precision=HIGHEST, preferred_element_type=F32),
     )
 
+    def spread(yy, c):
+        for b in range(half // 128):
+            tile = p2_all[yy, c, :, b * 128 : (b + 1) * 128]
+            high = tile.astype(BF16)
+            low = (tile - high.astype(F32)).astype(BF16)
+            start = yy * 2 * half + c * half + b * 128
+            p_rows[pl.ds(pl.multiple_of(start, 128), 128)] = jnp.concatenate([high, low, high, low], axis=0).T
+
+    for c in range(2):
+        spread(y, c)
+
     got(p2_all.at[pl.ds(0, ny - 1), 0], s_sem.at[2])
     for j in range(1, ny):
         theirs = p2_all.at[y_peer(j), core]
@@ -265,18 +312,9 @@
     at_the_end.append(lambda: sent(p2_all.at[pl.ds(0, ny - 1), 0], c_send_sem.at[2]))
     right, gram = summed_over_y(1)
     got(p2_all.at[pl.ds(0, ny - 1), 0], c_sem.at[2])
-
-    for yy in range(ny):
+    for j in range(1, ny):
         for c in range(2):
-
-            @pl.loop(0, half // 128)
-            def _(b):
-                tile = p2_all[yy, c, :, pl.ds(pl.multiple_of(b * 128, 128), 128)]
-                high = tile.astype(BF16)
-                low = (tile - high.astype(F32)).astype(BF16)
-                start = yy * 2 * half + c * half + b * 128
-                p_rows[pl.ds(pl.multiple_of(start, 128), 128)] = jnp.concatenate([high, low, high, low], axis=0).T
-
+            spread(y_peer(j), c)
     diagonal, lower, full = eliminate(gram, right, True)
     q_out[...] = lower / (jnp.sqrt(diagonal) * (ny * nz))
     m = full / (diagonal * (ny * nz))
@@ -284,7 +322,7 @@
     m_low = (m - m_high.astype(F32)).astype(BF16)
     m_rows = jnp.concatenate([m_high, m_high, m_low, m_low], axis=0)
 
-    @pl.loop(0, nz)
+    @pl.loop(0, nz, unroll=4)
     def _(i):
         zt = target(i)
         left = jnp.concatenate(
@@ -329,10 +367,10 @@
             pltpu.VMEM((ny, 2, RANK, half), F32),
             pltpu.VMEM((ny * nz * BLOCK, 4 * RANK), BF16),
             dma((2, nz)), dma, dma((PARTS, nz // GROUP)), dma, dma((PARTS,)), dma, dma, dma, dma, dma, dma,
-            dma((3,)), dma((3,)), dma((3,)), dma((3,)), dma, dma, dma,
+            dma((3,)), dma((3,)), dma((3,)), dma((3,)), dma, dma, dma, pltpu.SemaphoreType.REGULAR,
         ],
         compiler_params=pltpu.CompilerParams(
-            collective_id=0, has_side_effects=True, vmem_limit_bytes=60 * 1024 * 1024
+            collective_id=0, has_side_effects=True, vmem_limit_bytes=52 * 1024 * 1024
         ),
     )(grads.reshape(blocks), error.reshape(blocks), q_init.T)
     return new_error.reshape(1, ny * nz * BLOCK, COLS), q_rows.T

time: 84.7 us -> 74.4 us (0.88)
  Pallas kernels: 81 us -> 71.2 us
    pallas_call x1, Pallas kernels: 81 us -> 71.2 us  [on_device(): pl.pallas_call(functools.partial(kernel, ny, nz, nt), out_shape=(jax.Shap...]
where the time goes in v3:
time: 74.4 us; the launch traced here: 74.2 us
  Pallas kernels  71.2 us (96%)
  local copies, waits for them, and re-layouts  2.29 us (3%)
    pallas_call x1, Pallas kernels, on_device(): pl.pallas_call(functools.partial(kernel, ny, nz, nt), out_shape=(jax.Shap...  71.2 us
    unnamed x4, local copies, waits for them, and re-layouts  2.29 us

profile of v3, /device:TPU:1, one launch (start us, length us, event | category | flops | bytes accessed | tf_op | source)
XLA Modules:
  0.0 74.2 jit_solution(13784132906639426778)
XLA Ops:
  0.6 0.0 copy-start
  0.6 0.7 copy-done
  1.3 71.2 %shard_map.50 = (bf16[4,16,64,128]{3,2,1,0:T(8,128)(2,1)S(1)}, f32[32,128]{1,0:T(8,128)S(1)}) custom-call(bf16[4,16,64,128]{3,2,1,0:T(8,128)(2,1)} %bitcast.8, bf16[4,16,64,128]{3,2,1,0:T(8,128)(2,1)} %bitcast.9, f32[32,128]{1,0:T(8,128)S(1)} %bitcast.6), custom_call_target="tpu_custom_call" | custom-call | tf_op jit(solution)/shard_map/pallas_call | solution.py:344
  72.6 1.0 %copy.7 = bf16[1,4096,128]{2,1,0:T(8,128)(2,1)} copy(bf16[1,4096,128]{2,1,0:T(8,128)(2,1)S(1)} %bitcast.5) | data formatting | bytes 2097152
  73.6 0.6 copy.8
Async XLA Ops:
  0.6 0.7 copy-start

commit v4 on v3

--- a/solution.py
+++ b/solution.py
@@ -11,8 +11,8 @@
 HIGHEST = lax.Precision.HIGHEST
 RANK = 32
 BLOCK = 64
-PARTS = 2
-PART = BLOCK // PARTS
+CUTS = (0, 32, BLOCK)
+PARTS = len(CUTS) - 1
 STEPS = 8
 GROUP = 2
 COLS = 128
@@ -65,7 +65,7 @@
     grads, error, q_init, new_error, q_out,
     g_buf, e_buf, acc, y_buf, z_send, z_buf, a_all, t_buf, p1_all, s_buf, part_buf, c_buf, x_buf, p2_all, p_rows,
     load_sem, y_send_sem, y_sem, z_send_sem, z_sem, a_send_sem, a_sem, t_send_sem, t_sem, p_send_sem, p_sem,
-    s_send_sem, s_sem, c_send_sem, c_sem, x_send_sem, x_sem, store_sem, ready,
+    s_send_sem, s_sem, c_send_sem, c_sem, x_send_sem, x_sem, ready,
 ):
     nx = nt // 2
     dp, t = lax.axis_index("dp"), lax.axis_index("tensor")
@@ -108,14 +108,8 @@
     def enter(y_, z_, t_):
         pl.semaphore_signal(barrier, inc=1, device_id=(y_ * nz + z_, t_), device_id_type=MESH)
 
-    @pl.loop(0, nz - 1)
-    def _(i):
-        enter(y, target(i), x * 2 + 1)
-
     for j in range(1, ny):
         enter(y_peer(j), z, x * 2)
-    for j in range(1, nx):
-        enter(y, z, lax.rem(x + j, nx) * 2 + 1)
     enter(y, z, sibling)
 
     @pl.loop(0, nz)
@@ -123,16 +117,23 @@
         for load in loads(i):
             load.start()
 
+    @pl.loop(0, nz - 1)
+    def _(i):
+        enter(y, target(i), x * 2 + 1)
+
+    for j in range(1, nx):
+        enter(y, z, lax.rem(x + j, nx) * 2 + 1)
+
     at_the_end = []
 
     def rows_of(h):
-        return pl.ds(h * PART, PART)
+        return pl.ds(CUTS[h], CUTS[h + 1] - CUTS[h])
 
     def send_y(h, g):
         group = pl.ds(g * GROUP, GROUP)
         for j in range(1, ny):
             remote(
-                acc.at[group, y_peer(j), rows_of(h)], y_buf.at[h, group, j - 1],
+                acc.at[group, y_peer(j), rows_of(h)], y_buf.at[group, j - 1, rows_of(h)],
                 y_send_sem, y_sem.at[h, g], y_peer(j), z, t,
             ).start()
 
@@ -172,9 +173,9 @@
     at_the_end.append(lambda: sent(acc.at[:, pl.ds(0, ny - 1)], y_send_sem))
 
     def y_total(h, i):
-        total = acc[i, y, h * PART : (h + 1) * PART].astype(F32)
+        total = acc[i, y, rows_of(h)].astype(F32)
         for j in range(ny - 1):
-            total = total + y_buf[h, i, j].astype(F32)
+            total = total + y_buf[i, j, rows_of(h)].astype(F32)
         return total
 
     entered(1, 2 * (nz - 1) + 2 * (nx - 1) + 1)
@@ -183,22 +184,24 @@
 
         @pl.loop(0, nz // GROUP)
         def _(g):
-            got(y_buf.at[h, pl.ds(g * GROUP, GROUP)], y_sem.at[h, g])
+            got(y_buf.at[pl.ds(g * GROUP, GROUP), :, rows_of(h)], y_sem.at[h, g])
 
             @pl.loop(g * GROUP, lax.min((g + 1) * GROUP, nz - 1))
             def _(i):
-                z_send[h, i] = y_total(h, i).astype(BF16)
-                remote(z_send.at[h, i], z_buf.at[h, i], z_send_sem, z_sem.at[h], y, target(i), t).start()
+                z_send[i, rows_of(h)] = y_total(h, i).astype(BF16)
+                remote(
+                    z_send.at[i, rows_of(h)], z_buf.at[i, rows_of(h)], z_send_sem, z_sem.at[h], y, target(i), t
+                ).start()
 
         own.append(y_total(h, nz - 1))
     at_the_end.append(lambda: sent(z_send, z_send_sem))
 
     for h in range(PARTS):
-        got(z_buf.at[h], z_sem.at[h])
+        got(z_buf.at[:, rows_of(h)], z_sem.at[h])
         total = own[h]
         for i in range(nz - 1):
-            total = total + z_buf[h, i].astype(F32)
-        a_all[z, h * PART : (h + 1) * PART] = total.astype(BF16)
+            total = total + z_buf[i, rows_of(h)].astype(F32)
+        a_all[z, rows_of(h)] = total.astype(BF16)
         mine = a_all.at[z, rows_of(h)]
 
         @pl.loop(0, nz - 1)
@@ -287,12 +290,13 @@
     p2 = jnp.concatenate([p2_all[y, 0], p2_all[y, 1]], axis=1)
     p2_high = p2.astype(BF16)
     p2_low = (p2 - p2_high.astype(F32)).astype(BF16)
-    both = jnp.dot(jnp.concatenate([p2_high, p2_low], axis=0), a, preferred_element_type=F32)
-    sum_over_y(
-        1,
-        both[:RANK] + both[RANK:],
-        lax.dot_general(p2, p2, (((1,), (1,)), ((), ())), precision=HIGHEST, preferred_element_type=F32),
-    )
+    halves = jnp.concatenate([p2_high, p2_low], axis=0)
+
+    def with_halves(right, contract):
+        both = lax.dot_general(halves, right, (((1,), (contract,)), ((), ())), preferred_element_type=F32)
+        return both[:RANK] + both[RANK:]
+
+    sum_over_y(1, with_halves(a, 0), with_halves(p2_high, 1) + with_halves(p2_low, 1))
 
     def spread(yy, c):
         for b in range(half // 128):
@@ -329,12 +333,10 @@
             [p_rows[pl.ds(pl.multiple_of((yy * nz + zt) * BLOCK, BLOCK), BLOCK)] for yy in range(ny)], axis=0
         )
         approx = jnp.dot(left, m_rows, preferred_element_type=F32).reshape(ny, BLOCK, COLS)
-        g_buf[i] = (acc[i].astype(F32) - approx).astype(BF16)
-        pltpu.make_async_copy(g_buf.at[i], new_error.at[:, zt], store_sem).start()
+        new_error[:, zt] = (acc[i].astype(F32) - approx).astype(BF16)
 
     for wait in at_the_end:
         wait()
-    pltpu.make_async_copy(g_buf, g_buf, store_sem).wait()
 
 
 def on_device(ny, nz, nt, grads, error, q_init):
@@ -349,14 +351,14 @@
             pl.BlockSpec(memory_space=pl.ANY),
             pl.BlockSpec(memory_space=pltpu.VMEM),
         ],
-        out_specs=(pl.BlockSpec(memory_space=pl.ANY), pl.BlockSpec(memory_space=pltpu.VMEM)),
+        out_specs=(pl.BlockSpec(memory_space=pltpu.VMEM), pl.BlockSpec(memory_space=pltpu.VMEM)),
         scratch_shapes=[
             pltpu.VMEM((nz, ny, BLOCK, COLS), BF16),
             pltpu.VMEM((nz, ny, BLOCK, COLS), BF16),
             pltpu.VMEM((nz, ny, BLOCK, COLS), BF16),
-            pltpu.VMEM((PARTS, nz, ny - 1, PART, COLS), BF16),
-            pltpu.VMEM((PARTS, nz - 1, PART, COLS), BF16),
-            pltpu.VMEM((PARTS, nz - 1, PART, COLS), BF16),
+            pltpu.VMEM((nz, ny - 1, BLOCK, COLS), BF16),
+            pltpu.VMEM((nz - 1, BLOCK, COLS), BF16),
+            pltpu.VMEM((nz - 1, BLOCK, COLS), BF16),
             pltpu.VMEM((nz, BLOCK, COLS), BF16),
             pltpu.VMEM((nt, RANK // 2, 128), F32),
             pltpu.VMEM((nz, RANK // 2, 128), BF16),
@@ -367,7 +369,7 @@
             pltpu.VMEM((ny, 2, RANK, half), F32),
             pltpu.VMEM((ny * nz * BLOCK, 4 * RANK), BF16),
             dma((2, nz)), dma, dma((PARTS, nz // GROUP)), dma, dma((PARTS,)), dma, dma, dma, dma, dma, dma,
-            dma((3,)), dma((3,)), dma((3,)), dma((3,)), dma, dma, dma, pltpu.SemaphoreType.REGULAR,
+            dma((3,)), dma((3,)), dma((3,)), dma((3,)), dma, dma, pltpu.SemaphoreType.REGULAR,
         ],
         compiler_params=pltpu.CompilerParams(
             collective_id=0, has_side_effects=True, vmem_limit_bytes=52 * 1024 * 1024

time: 74.4 us -> 72.2 us (0.970)
  Pallas kernels: 71.2 us -> 69 us
    pallas_call x1, Pallas kernels: 71.2 us -> 69 us  [on_device(): pl.pallas_call(functools.partial(kernel, ny, nz, nt), out_shape=(jax.Shap...]
where the time goes in v4:
time: 72.2 us; the launch traced here: 71.9 us
  Pallas kernels  69 us (96%)
  local copies, waits for them, and re-layouts  2.29 us (3%)
    pallas_call x1, Pallas kernels, on_device(): pl.pallas_call(functools.partial(kernel, ny, nz, nt), out_shape=(jax.Shap...  69 us
    unnamed x4, local copies, waits for them, and re-layouts  2.29 us

profile of v4, /device:TPU:1, one launch (start us, length us, event | category | flops | bytes accessed | tf_op | source)
XLA Modules:
  0.0 71.9 jit_solution(12065178806786044234)
XLA Ops:
  0.6 0.0 copy-start
  0.6 0.7 copy-done
  1.3 69.0 %shard_map.50 = (bf16[4,16,64,128]{3,2,1,0:T(8,128)(2,1)S(1)}, f32[32,128]{1,0:T(8,128)S(1)}) custom-call(bf16[4,16,64,128]{3,2,1,0:T(8,128)(2,1)} %bitcast.8, bf16[4,16,64,128]{3,2,1,0:T(8,128)(2,1)} %bitcast.9, f32[32,128]{1,0:T(8,128)S(1)} %bitcast.6), custom_call_target="tpu_custom_call" | custom-call | tf_op jit(solution)/shard_map/pallas_call | solution.py:346
  70.3 1.0 %copy.7 = bf16[1,4096,128]{2,1,0:T(8,128)(2,1)} copy(bf16[1,4096,128]{2,1,0:T(8,128)(2,1)S(1)} %bitcast.5) | data formatting | bytes 2097152
  71.3 0.6 copy.8
Async XLA Ops:
  0.6 0.7 copy-start

commit v5 on v4

--- a/solution.py
+++ b/solution.py
@@ -64,7 +64,7 @@
     ny, nz, nt,
     grads, error, q_init, new_error, q_out,
     g_buf, e_buf, acc, y_buf, z_send, z_buf, a_all, t_buf, p1_all, s_buf, part_buf, c_buf, x_buf, p2_all, p_rows,
-    load_sem, y_send_sem, y_sem, z_send_sem, z_sem, a_send_sem, a_sem, t_send_sem, t_sem, p_send_sem, p_sem,
+    load_sem, y_send_sem, y_sem, z_send_sem, z_sem, a_send_sem, a_sem, n_send_sem, n_sem, t_send_sem, t_sem, p_send_sem, p_sem,
     s_send_sem, s_sem, c_send_sem, c_sem, x_send_sem, x_sem, ready,
 ):
     nx = nt // 2
@@ -196,23 +196,26 @@
         own.append(y_total(h, nz - 1))
     at_the_end.append(lambda: sent(z_send, z_send_sem))
 
+    turns = nz // 4
+    turn, kind = lax.div(z, 4), lax.rem(z, 4)
+
+    def z_near(j):
+        return lax.rem(z + j + nz, nz)
+
     for h in range(PARTS):
         got(z_buf.at[:, rows_of(h)], z_sem.at[h])
         total = own[h]
         for i in range(nz - 1):
             total = total + z_buf[i, rows_of(h)].astype(F32)
-        a_all[z, rows_of(h)] = total.astype(BF16)
-        mine = a_all.at[z, rows_of(h)]
-
-        @pl.loop(0, nz - 1)
-        def _(i):
-            remote(mine, mine, a_send_sem, a_sem, y, target(i), t).start()
-
-    at_the_end.append(lambda: sent(a_all.at[pl.ds(0, nz - 1)], a_send_sem))
+        a_all[kind, turn, rows_of(h)] = total.astype(BF16)
+        mine = a_all.at[kind, turn, rows_of(h)]
+        for j in range(1, turns):
+            remote(mine, mine, a_send_sem, a_sem.at[h], y, z_near(4 * j), t).start()
+    at_the_end.append(lambda: sent(a_all.at[0, pl.ds(0, turns - 1)], a_send_sem))
 
     lane16 = lax.broadcasted_iota(jnp.int32, (RANK // 2, 128), 1)
     q_rows = q_init[...].astype(BF16)
-    block = a_all[z]
+    block = a_all[kind, turn]
     p_part = lax.dot_general(
         q_rows, jnp.concatenate([block, block], axis=0), (((1,), (1,)), ((), ())), preferred_element_type=F32
     )
@@ -224,14 +227,21 @@
     p_packed = t_buf[0]
     for j in range(1, nt):
         p_packed = p_packed + t_buf[j]
-    p1_all[z] = p_packed.astype(BF16)
+    p1_own = p1_all.at[kind * turns + turn]
+    p1_own[...] = p_packed.astype(BF16)
 
     @pl.loop(0, nz - 1)
     def _(i):
-        remote(p1_all.at[z], p1_all.at[z], p_send_sem, p_sem, y, target(i), t).start()
+        remote(p1_own, p1_own, p_send_sem, p_sem, y, target(i), t).start()
 
     at_the_end.append(lambda: sent(p1_all.at[pl.ds(0, nz - 1)], p_send_sem))
-    got(a_all.at[pl.ds(0, nz - 1)], a_sem)
+    for h in range(PARTS):
+        got(a_all.at[0, pl.ds(0, turns - 1), rows_of(h)], a_sem.at[h])
+        for near, first, count in ((2, 0, turns // 2), (-2, turns // 2, turns // 2), (1, 0, turns), (-1, 0, turns)):
+            some = a_all.at[kind, pl.ds(first, count), rows_of(h)]
+            remote(some, some, n_send_sem, n_sem, y, z_near(near), t).start()
+    at_the_end.append(lambda: sent(a_all.at[pl.ds(0, 3)], n_send_sem))
+    got(a_all.at[pl.ds(0, 3)], n_sem)
     got(p1_all.at[pl.ds(0, nz - 1)], p_sem)
     a = a_all[...].reshape(nz * BLOCK, COLS)
     columns = []
@@ -329,8 +339,9 @@
     @pl.loop(0, nz, unroll=4)
     def _(i):
         zt = target(i)
+        place = lax.rem(zt, 4) * (nz // 4) + lax.div(zt, 4)
         left = jnp.concatenate(
-            [p_rows[pl.ds(pl.multiple_of((yy * nz + zt) * BLOCK, BLOCK), BLOCK)] for yy in range(ny)], axis=0
+            [p_rows[pl.ds(pl.multiple_of((yy * nz + place) * BLOCK, BLOCK), BLOCK)] for yy in range(ny)], axis=0
         )
         approx = jnp.dot(left, m_rows, preferred_element_type=F32).reshape(ny, BLOCK, COLS)
         new_error[:, zt] = (acc[i].astype(F32) - approx).astype(BF16)
@@ -359,7 +370,7 @@
             pltpu.VMEM((nz, ny - 1, BLOCK, COLS), BF16),
             pltpu.VMEM((nz - 1, BLOCK, COLS), BF16),
             pltpu.VMEM((nz - 1, BLOCK, COLS), BF16),
-            pltpu.VMEM((nz, BLOCK, COLS), BF16),
+            pltpu.VMEM((4, nz // 4, BLOCK, COLS), BF16),
             pltpu.VMEM((nt, RANK // 2, 128), F32),
             pltpu.VMEM((nz, RANK // 2, 128), BF16),
             pltpu.VMEM((2, ny, SUMS, 128), F32),
@@ -368,7 +379,7 @@
             pltpu.VMEM((nt // 2, RANK, half), F32),
             pltpu.VMEM((ny, 2, RANK, half), F32),
             pltpu.VMEM((ny * nz * BLOCK, 4 * RANK), BF16),
-            dma((2, nz)), dma, dma((PARTS, nz // GROUP)), dma, dma((PARTS,)), dma, dma, dma, dma, dma, dma,
+            dma((2, nz)), dma, dma((PARTS, nz // GROUP)), dma, dma((PARTS,)), dma, dma((PARTS,)), dma, dma, dma, dma, dma, dma,
             dma((3,)), dma((3,)), dma((3,)), dma((3,)), dma, dma, pltpu.SemaphoreType.REGULAR,
         ],
         compiler_params=pltpu.CompilerParams(

time: 72.2 us -> 68.7 us (0.952)
  Pallas kernels: 69 us -> 65.5 us
    pallas_call x1, Pallas kernels: 69 us -> 65.5 us  [on_device(): pl.pallas_call(functools.partial(kernel, ny, nz, nt), out_shape=(jax.Shap...]
where the time goes in v5:
time: 68.7 us; the launch traced here: 68.5 us
  Pallas kernels  65.5 us (95%)
  local copies, waits for them, and re-layouts  2.29 us (3%)
    pallas_call x1, Pallas kernels, on_device(): pl.pallas_call(functools.partial(kernel, ny, nz, nt), out_shape=(jax.Shap...  65.5 us
    unnamed x4, local copies, waits for them, and re-layouts  2.29 us

profile of v5, /device:TPU:1, one launch (start us, length us, event | category | flops | bytes accessed | tf_op | source)
XLA Modules:
  0.0 68.5 jit_solution(13360427652800385665)
XLA Ops:
  0.6 0.0 copy-start
  0.6 0.7 %copy-done = f32[128,32]{0,1:T(8,128)S(1)} copy-done((f32[128,32]{0,1:T(8,128)S(1)}, f32[128,32]{0,1:T(8,128)}, u32[]{:S(2)}) %copy-start) | copy-done | bytes 16408
  1.3 65.5 %shard_map.50 = (bf16[4,16,64,128]{3,2,1,0:T(8,128)(2,1)S(1)}, f32[32,128]{1,0:T(8,128)S(1)}) custom-call(bf16[4,16,64,128]{3,2,1,0:T(8,128)(2,1)} %bitcast.8, bf16[4,16,64,128]{3,2,1,0:T(8,128)(2,1)} %bitcast.9, f32[32,128]{1,0:T(8,128)S(1)} %bitcast.6), custom_call_target="tpu_custom_call" | custom-call | tf_op jit(solution)/shard_map/pallas_call | solution.py:357
  66.9 1.0 %copy.7 = bf16[1,4096,128]{2,1,0:T(8,128)(2,1)} copy(bf16[1,4096,128]{2,1,0:T(8,128)(2,1)S(1)} %bitcast.5) | data formatting | bytes 2097152
  67.9 0.6 copy.8
Async XLA Ops:
  0.6 0.7 %copy-start = (f32[128,32]{0,1:T(8,128)S(1)}, f32[128,32]{0,1:T(8,128)}, u32[]{:S(2)}) copy-start(f32[128,32]{0,1:T(8,128)} %param.5) | copy-start | bytes 49156

commit v6 on v5

--- a/solution.py
+++ b/solution.py
@@ -126,6 +126,10 @@
 
     at_the_end = []
 
+    def all_sent():
+        while at_the_end:
+            at_the_end.pop(0)()
+
     def rows_of(h):
         return pl.ds(CUTS[h], CUTS[h + 1] - CUTS[h])
 
@@ -266,11 +270,15 @@
             total = total + s_buf[it, j]
         return total[:RANK], total[RANK:]
 
+    before = list(at_the_end)
+    at_the_end.clear()
     sum_over_y(
         0,
         jnp.dot(p1, a, preferred_element_type=F32),
         lax.dot_general(p1, p1, (((1,), (1,)), ((), ())), preferred_element_type=F32),
     )
+    for wait in before:
+        wait()
     right, gram = summed_over_y(0)
     diagonal, lower, _ = eliminate(gram, right, False)
     q_rows = (lower / (jnp.sqrt(diagonal) * (ny * nz))).astype(BF16)
@@ -281,43 +289,42 @@
     remote(part_buf.at[other], c_buf, c_send_sem.at[0], c_sem.at[0], y, z, sibling).start()
     at_the_end.append(lambda: sent(c_buf, c_send_sem.at[0]))
     got(c_buf, c_sem.at[0])
-    x_buf[x] = part_buf[core] + c_buf[...]
+    x_buf[x] = (part_buf[core] + c_buf[...]).astype(BF16)
     for j in range(1, nx):
         remote(x_buf.at[x], x_buf.at[x], x_send_sem, x_sem, y, z, lax.rem(x + j, nx) * 2 + core).start()
+    all_sent()
     at_the_end.append(lambda: sent(x_buf.at[pl.ds(0, nx - 1)], x_send_sem))
     got(x_buf.at[pl.ds(0, nx - 1)], x_sem)
-    p_half = x_buf[0]
+    before = list(at_the_end)
+    at_the_end.clear()
+    p_half = x_buf[0].astype(F32)
     for j in range(1, nx):
-        p_half = p_half + x_buf[j]
-    p2_all[y, core] = p_half
+        p_half = p_half + x_buf[j].astype(F32)
+    p2_all[y, core] = p_half.astype(BF16)
     mine = p2_all.at[y, core]
     remote(mine, mine, c_send_sem.at[1], c_sem.at[1], y, z, sibling).start()
-    at_the_end.append(lambda: sent(c_buf, c_send_sem.at[1]))
+    at_the_end.append(lambda: sent(mine, c_send_sem.at[1]))
     for j in range(1, ny):
         remote(mine, mine, s_send_sem.at[2], s_sem.at[2], y_peer(j), z, t).start()
     at_the_end.append(lambda: sent(p2_all.at[pl.ds(0, ny - 1), 0], s_send_sem.at[2]))
     got(p2_all.at[y, other], c_sem.at[1])
     p2 = jnp.concatenate([p2_all[y, 0], p2_all[y, 1]], axis=1)
-    p2_high = p2.astype(BF16)
-    p2_low = (p2 - p2_high.astype(F32)).astype(BF16)
-    halves = jnp.concatenate([p2_high, p2_low], axis=0)
-
-    def with_halves(right, contract):
-        both = lax.dot_general(halves, right, (((1,), (contract,)), ((), ())), preferred_element_type=F32)
-        return both[:RANK] + both[RANK:]
-
-    sum_over_y(1, with_halves(a, 0), with_halves(p2_high, 1) + with_halves(p2_low, 1))
+    sum_over_y(
+        1,
+        jnp.dot(p2, a, preferred_element_type=F32),
+        lax.dot_general(p2, p2, (((1,), (1,)), ((), ())), preferred_element_type=F32),
+    )
 
     def spread(yy, c):
         for b in range(half // 128):
             tile = p2_all[yy, c, :, b * 128 : (b + 1) * 128]
-            high = tile.astype(BF16)
-            low = (tile - high.astype(F32)).astype(BF16)
             start = yy * 2 * half + c * half + b * 128
-            p_rows[pl.ds(pl.multiple_of(start, 128), 128)] = jnp.concatenate([high, low, high, low], axis=0).T
+            p_rows[pl.ds(pl.multiple_of(start, 128), 128)] = jnp.concatenate([tile] * 4, axis=0).T
 
     for c in range(2):
         spread(y, c)
+    for wait in before:
+        wait()
 
     got(p2_all.at[pl.ds(0, ny - 1), 0], s_sem.at[2])
     for j in range(1, ny):
@@ -334,7 +341,7 @@
     m = full / (diagonal * (ny * nz))
     m_high = m.astype(BF16)
     m_low = (m - m_high.astype(F32)).astype(BF16)
-    m_rows = jnp.concatenate([m_high, m_high, m_low, m_low], axis=0)
+    m_rows = jnp.concatenate([m_high, m_low, jnp.zeros_like(m_high), jnp.zeros_like(m_high)], axis=0)
 
     @pl.loop(0, nz, unroll=4)
     def _(i):
@@ -346,8 +353,7 @@
         approx = jnp.dot(left, m_rows, preferred_element_type=F32).reshape(ny, BLOCK, COLS)
         new_error[:, zt] = (acc[i].astype(F32) - approx).astype(BF16)
 
-    for wait in at_the_end:
-        wait()
+    all_sent()
 
 
 def on_device(ny, nz, nt, grads, error, q_init):
@@ -376,8 +382,8 @@
             pltpu.VMEM((2, ny, SUMS, 128), F32),
             pltpu.VMEM((2, RANK, half), F32),
             pltpu.VMEM((RANK, half), F32),
-            pltpu.VMEM((nt // 2, RANK, half), F32),
-            pltpu.VMEM((ny, 2, RANK, half), F32),
+            pltpu.VMEM((nt // 2, RANK, half), BF16),
+            pltpu.VMEM((ny, 2, RANK, half), BF16),
             pltpu.VMEM((ny * nz * BLOCK, 4 * RANK), BF16),
             dma((2, nz)), dma, dma((PARTS, nz // GROUP)), dma, dma((PARTS,)), dma, dma((PARTS,)), dma, dma, dma, dma, dma, dma,
             dma((3,)), dma((3,)), dma((3,)), dma((3,)), dma, dma, pltpu.SemaphoreType.REGULAR,

time: 68.7 us -> 65.7 us (0.956)
  Pallas kernels: 65.5 us -> 62.5 us
    pallas_call x1, Pallas kernels: 65.5 us -> 62.5 us  [on_device(): pl.pallas_call(functools.partial(kernel, ny, nz, nt), out_shape=(jax.Shap...]
where the time goes in v6:
time: 65.7 us; the launch traced here: 65.5 us
  Pallas kernels  62.5 us (95%)
  local copies, waits for them, and re-layouts  2.29 us (3%)
    pallas_call x1, Pallas kernels, on_device(): pl.pallas_call(functools.partial(kernel, ny, nz, nt), out_shape=(jax.Shap...  62.5 us
    unnamed x4, local copies, waits for them, and re-layouts  2.29 us

profile of v6, /device:TPU:1, one launch (start us, length us, event | category | flops | bytes accessed | tf_op | source)
XLA Modules:
  0.0 65.5 jit_solution(13135472991876666426)
XLA Ops:
  0.6 0.0 copy-start
  0.6 0.7 %copy-done = f32[128,32]{0,1:T(8,128)S(1)} copy-done((f32[128,32]{0,1:T(8,128)S(1)}, f32[128,32]{0,1:T(8,128)}, u32[]{:S(2)}) %copy-start) | copy-done | bytes 16408
  1.3 62.5 %shard_map.50 = (bf16[4,16,64,128]{3,2,1,0:T(8,128)(2,1)S(1)}, f32[32,128]{1,0:T(8,128)S(1)}) custom-call(bf16[4,16,64,128]{3,2,1,0:T(8,128)(2,1)} %bitcast.8, bf16[4,16,64,128]{3,2,1,0:T(8,128)(2,1)} %bitcast.9, f32[32,128]{1,0:T(8,128)S(1)} %bitcast.6), custom_call_target="tpu_custom_call" | custom-call | tf_op jit(solution)/shard_map/pallas_call | solution.py:363
  63.9 1.0 %copy.7 = bf16[1,4096,128]{2,1,0:T(8,128)(2,1)} copy(bf16[1,4096,128]{2,1,0:T(8,128)(2,1)S(1)} %bitcast.5) | data formatting | bytes 2097152
  64.8 0.6 copy.8
Async XLA Ops:
  0.6 0.7 %copy-start = (f32[128,32]{0,1:T(8,128)S(1)}, f32[128,32]{0,1:T(8,128)}, u32[]{:S(2)}) copy-start(f32[128,32]{0,1:T(8,128)} %param.5) | copy-start | bytes 49156
